TPU v7x, 32 devices: a whole 2x2x4 slice. The times are simulated.
32 devices in a mesh: groups: 2 (over x), face: 8 (over z, y), tile: 2 (over core).
Axes of the slice: x: 2, y: 2, z: 4, core: 2. Of those that a mesh axis runs over, the one named last changes fastest.
Arguments:
- fields: float32 [32, 64, 128, 128], P(('groups', 'face'), None, 'tile'), parts along dimension 0, may hold values from -8 to 8
- cotangent: float32 [32, 64, 128, 128], P(('groups', 'face'), None, 'tile'), parts along dimension 0, may hold values from -0.125 to 0.125
- first_kernel: float32 [64, 64, 3, 3], replicated, may hold values from -0.25 to 0.25
- second_kernel: float32 [64, 64, 3, 3], replicated, may hold values from -0.25 to 0.25
- coarse_kernel: float32 [64, 64, 3, 3], replicated, may hold values from -0.25 to 0.25
- slot_faces: int32 [16], replicated, may hold values from -1 to 11, as said below
- edge_table: int32 [16, 4, 2], replicated, may hold values from 0 to 15, as said below
- corner_table: int32 [16, 4, 3], replicated, may hold values from 0 to 15, as said below
Outputs:
- section_output: float32 [32, 64, 128, 128], P(('groups', 'face'), None, 'tile'), parts along dimension 0
- grad_first: float32 [128, 64, 3, 3], P('groups'), parts along dimension 0
- grad_second: float32 [128, 64, 3, 3], P('groups'), parts along dimension 0
- grad_coarse: float32 [128, 64, 3, 3], P('groups'), parts along dimension 0
There are 2 independent parts, one for each index of `groups`. A program takes and returns all parts, laid end to end along the dimension named above; an argument that names none is the same for every part. Nothing has to cross between parts.
Inputs may be any that keep to these rules, and one draw needn't show every extreme that they name: `slot_faces`: each face 0 to 11 stands in exactly one slot; the other slots hold -1. `edge_table`: for an occupied slot the entries follow the HEALPix base tessellation under the slot map; an empty slot names itself and its own side. The relation is symmetric: if side s of slot q names side t of slot p, then side t of p names side s of q. `corner_table`: entry [q, k, 2] is 1 where a fourth face meets diagonally at corner k, else 0 and the entry names slot q and corner k itself; empty slots name themselves. The relation is symmetric: if corner k of q names corner m of p, then corner m of p names corner k of q.
All inputs are finite; a program needn't handle non-finite values.
Results may differ from a plain program's by a relative error of at most 0.0003.
Values sent between devices are 32-bit elements; how exact they have to be, the bound alone decides.
A program may use at most 256 MiB of HBM per device.

v0:
```python
from functools import partial
import jax
import jax.numpy as jnp
from jax import lax
from jax.sharding import PartitionSpec as P

BLOCK = 4


def convolve(padded, kernel):
    return lax.conv_general_dilated(padded, kernel, (1, 1), "VALID", precision=lax.Precision.HIGH)


def activate(values):
    return jax.nn.gelu(values, approximate=False)


def activation_grad(values, grads):
    return jax.vjp(activate, lax.optimization_barrier(values))[1](grads)[0]


def split_sum(values, devices):
    turned = values.transpose(2, 3, 1, 0)
    shares = turned.reshape(devices, -1, 128)
    share = lax.psum_scatter(shares, ("face", "tile"), scatter_dimension=0, tiled=True)
    whole = lax.all_gather(share, ("face", "tile"), axis=0, tiled=True)
    return whole.reshape(turned.shape).transpose(3, 2, 0, 1)


def rim_pieces(tile_field):
    last_row = tile_field.shape[2] - 1
    last_col = tile_field.shape[3] - 1
    columns = jnp.stack([tile_field[:, :, :, 0], tile_field[:, :, :, last_col]], axis=1)[None]
    borders = jnp.stack([tile_field[:, :, 0, :], tile_field[:, :, last_row, :]], axis=1)[None]
    return (columns, borders)


def fine_gather(tile_field):
    columns, borders = rim_pieces(tile_field)
    tile_rows = columns.shape[-1]
    both = lax.all_gather(
        jnp.concatenate([columns, borders], axis=-1), ("face", "tile"), axis=0, tiled=True
    )
    return (both[..., :tile_rows], both[..., tile_rows:])


def fine_return(grad_columns, grad_borders):
    tile_rows = grad_columns.shape[-1]
    both = lax.psum_scatter(
        jnp.concatenate([grad_columns, grad_borders], axis=-1),
        ("face", "tile"),
        scatter_dimension=0,
        tiled=True,
    )
    return (both[..., :tile_rows], both[..., tile_rows:])


def fetch_lines(
    columns_all, borders_all, face_index, tile_index, face_count, tile_count, my_edges, my_corners
):
    slots_dev = columns_all.shape[1]
    channels = columns_all.shape[3]
    tile_rows = columns_all.shape[4]
    length = borders_all.shape[-1]
    cols_all = columns_all.reshape(face_count, tile_count, slots_dev, 2, channels, tile_rows)
    bord_all = borders_all.reshape(face_count, tile_count, slots_dev, 2, channels, length)
    near_slot = my_edges[:, :, 0]
    near_side = my_edges[:, :, 1]
    near_face = near_slot // slots_dev
    near_local = near_slot % slots_dev
    col_pick = jnp.where(near_side == 1, 1, 0)
    col_lines = cols_all[near_face, :, near_local, col_pick]
    col_lines = col_lines.transpose(0, 1, 3, 2, 4).reshape(
        slots_dev, 4, channels, tile_count * tile_rows
    )
    row_tile = jnp.where(near_side == 0, 0, tile_count - 1)
    row_pick = jnp.where(near_side == 0, 0, 1)
    row_lines = bord_all[near_face, row_tile, near_local, row_pick]
    halo_lines = jnp.where((near_side % 2 == 1)[:, :, None, None], col_lines, row_lines)
    corner_slot = my_corners[:, :, 0]
    corner_kind = my_corners[:, :, 1]
    corner_face = corner_slot // slots_dev
    corner_local = corner_slot % slots_dev
    corner_tile = jnp.where(corner_kind < 2, 0, tile_count - 1)
    corner_row = jnp.where(corner_kind < 2, 0, 1)
    corner_col = jnp.where((corner_kind == 0) | (corner_kind == 3), 0, length - 1)
    picked = bord_all[corner_face, corner_tile, corner_local, corner_row, :, corner_col]
    above_tile = bord_all[face_index, jnp.maximum(tile_index - 1, 0), :, 1]
    below_tile = bord_all[face_index, jnp.minimum(tile_index + 1, tile_count - 1), :, 0]
    return (halo_lines, picked, above_tile, below_tile)


def assemble(tile_field, pieces, tile_index, tile_count, my_corners):
    halo_lines, picked, above_tile, below_tile = pieces
    tile_rows = tile_field.shape[2]
    corner_flag = my_corners[:, :, 2]
    south_east = halo_lines[:, 0]
    north_east = halo_lines[:, 1]
    north_west = halo_lines[:, 2]
    south_west = halo_lines[:, 3]
    averaged = jnp.stack(
        [
            0.5 * (south_east[..., 0] + south_west[..., 0]),
            0.5 * (south_east[..., -1] + north_east[..., 0]),
            0.5 * (north_west[..., -1] + north_east[..., -1]),
            0.5 * (north_west[..., 0] + south_west[..., -1]),
        ],
        axis=1,
    )
    corners = jnp.where((corner_flag == 1)[:, :, None], picked, averaged)
    west_line = jnp.concatenate(
        [corners[:, 0, :, None], south_west, corners[:, 3, :, None]], axis=-1
    )
    east_line = jnp.concatenate(
        [corners[:, 1, :, None], north_east, corners[:, 2, :, None]], axis=-1
    )
    west_part = lax.dynamic_slice_in_dim(west_line, tile_index * tile_rows, tile_rows + 2, axis=2)
    east_part = lax.dynamic_slice_in_dim(east_line, tile_index * tile_rows, tile_rows + 2, axis=2)
    above_row = jnp.where(tile_index == 0, south_east, above_tile)
    below_row = jnp.where(tile_index == tile_count - 1, north_west, below_tile)
    top_row = jnp.concatenate([west_part[..., :1], above_row, east_part[..., :1]], axis=-1)
    bottom = jnp.concatenate([west_part[..., -1:], below_row, east_part[..., -1:]], axis=-1)
    middle = jnp.concatenate(
        [west_part[..., 1:-1, None], tile_field, east_part[..., 1:-1, None]], axis=-1
    )
    return jnp.concatenate([top_row[:, :, None], middle, bottom[:, :, None]], axis=2)


def framed_tile(
    tile_field,
    columns_all,
    borders_all,
    face_index,
    tile_index,
    face_count,
    tile_count,
    my_edges,
    my_corners,
):
    pieces = fetch_lines(
        columns_all,
        borders_all,
        face_index,
        tile_index,
        face_count,
        tile_count,
        my_edges,
        my_corners,
    )
    return assemble(tile_field, pieces, tile_index, tile_count, my_corners)


def local(
    fields,
    cotangent,
    first_kernel,
    second_kernel,
    coarse_kernel,
    slot_faces,
    edge_table,
    corner_table,
):
    face_index = lax.axis_index("face")
    tile_index = lax.axis_index("tile")
    face_count = lax.axis_size("face")
    tile_count = lax.axis_size("tile")
    slots_dev = fields.shape[0]
    my_slots = face_index * slots_dev + jnp.arange(slots_dev, dtype=jnp.int32)
    my_edges = edge_table[my_slots]
    my_corners = corner_table[my_slots]
    occupied = (slot_faces[my_slots] >= 0).astype(jnp.float32)[:, None, None, None]
    framer = partial(
        framed_tile,
        face_index=face_index,
        tile_index=tile_index,
        face_count=face_count,
        tile_count=tile_count,
        my_edges=my_edges,
        my_corners=my_corners,
    )
    columns_in, borders_in = fine_gather(fields)
    padded_in = framer(fields, columns_in, borders_in)
    first_act = convolve(padded_in, first_kernel)
    hidden = activate(first_act)
    columns_mid, borders_mid = fine_gather(hidden)
    padded_mid, frame_pull = jax.vjp(framer, hidden, columns_mid, borders_mid)
    second_act, second_pull = jax.vjp(convolve, padded_mid, second_kernel)
    features = activate(second_act)
    channels = features.shape[1]
    tile_rows = features.shape[2]
    length = features.shape[3]
    coarse = features.reshape(
        slots_dev, channels, tile_rows // BLOCK, BLOCK, length // BLOCK, BLOCK
    ).mean(axis=(3, 5))
    columns_low, borders_low = fine_gather(coarse)
    padded_low, low_pull = jax.vjp(framer, coarse, columns_low, borders_low)
    coarse_act, coarse_pull = jax.vjp(convolve, padded_low, coarse_kernel)
    bottleneck, bottleneck_pull = jax.vjp(activate, coarse_act)
    widened = jnp.repeat(jnp.repeat(bottleneck, BLOCK, axis=2), BLOCK, axis=3)
    section_output = (features + widened) * occupied
    masked = cotangent * occupied
    grad_bottleneck = masked.reshape(
        slots_dev, channels, tile_rows // BLOCK, BLOCK, length // BLOCK, BLOCK
    ).sum(axis=(3, 5))
    (grad_coarse_act,) = bottleneck_pull(grad_bottleneck)
    grad_padded_low, grad_coarse = coarse_pull(grad_coarse_act)
    grad_local, grad_columns_low, grad_borders_low = low_pull(grad_padded_low)
    back_low = fine_return(grad_columns_low, grad_borders_low)
    (spread_low,) = jax.vjp(rim_pieces, coarse)[1](back_low)
    grad_low = grad_local + spread_low
    grad_features = masked + jnp.repeat(jnp.repeat(grad_low, BLOCK, axis=2), BLOCK, axis=3) / (
        BLOCK * BLOCK
    )
    grad_second_act = activation_grad(second_act, grad_features)
    grad_padded_mid, grad_second = second_pull(grad_second_act)
    grad_hidden_local, grad_columns_mid, grad_borders_mid = frame_pull(grad_padded_mid)
    back_mid = fine_return(grad_columns_mid, grad_borders_mid)
    (spread_mid,) = jax.vjp(rim_pieces, hidden)[1](back_mid)
    grad_hidden = grad_hidden_local + spread_mid
    grad_second, grad_hidden = lax.optimization_barrier((grad_second, grad_hidden))
    grad_first_act = activation_grad(first_act, grad_hidden)
    (grad_first,) = jax.vjp(partial(convolve, padded_in), first_kernel)[1](grad_first_act)
    grad_second, grad_coarse = lax.psum((grad_second, grad_coarse), ("face", "tile"))
    grad_first = split_sum(grad_first, face_count * tile_count)
    return (section_output, grad_first, grad_second, grad_coarse)


def solution(mesh):
    in_specs = (
        P(("groups", "face"), None, "tile", None),
        P(("groups", "face"), None, "tile", None),
        P(),
        P(),
        P(),
        P(),
        P(),
        P(),
    )
    out_specs = (
        P(("groups", "face"), None, "tile", None),
        P("groups", None, None, None),
        P("groups", None, None, None),
        P("groups", None, None, None),
    )
    return jax.shard_map(local, mesh=mesh, in_specs=in_specs, out_specs=out_specs, check_vma=False)
```

profile of v0, /device:TPU:0, one launch (start us, length us, event | category | flops | bytes accessed | tf_op | source)
XLA Modules:
  0.0 1057.5 jit_solution(6484097872183846274)
XLA Ops:
  23.6 8.4 copy.804
  34.7 42.5 %all-gather.3.cloned.1.call-done = f32[16,2,2,64,192]{4,3,2,1,0:T(8,128)} async-done(((f32[1,2,2,64,192]{4,3,2,1,0:T(8,128)}), f32[16,2,2,64,192]{4,3,2,1,0:T(8,128)}) %all-gather.3.cloned.1.call-update) | async-done | bytes 3145744 | tf_op jit(solution)/shard_map/all_gather | solution.py:41
  91.8 28.1 %fusion.217 = f32[64,66,2,130]{0,2,3,1:T(2,128)S(1)} fusion(f32[2,64,1,130]{1,0,3,2:T(2,128)S(1)} %maximum_bitcast_fusion.2, f32[2,64,64,1]{1,0,3,2:T(2,128)S(1)} %slice_bitcast_fusion.17, f32[2,64,64,128]{1,0,3,2:T(2,128)} %copy.804, f32[2,64,64,1]{1,0,3,2:T(2,128)S(1)} %slice_bitcast_fusion.18, f32[2,64,1,130]{1,0,3,2:T(2,128)S(1)} %maximum_bitcast_fusion.1), kind=kLoop, calls=%fused_computation.508 | loop fusion | flops 4392960 | bytes 8785920 | tf_op jit(solution)/shard_map/concatenate | solution.py:126
  124.5 72.1 %fusion.13 = (f32[64,16,17,64]{3,1,2,0:T(8,128)S(1)}, f32[64,16,17,64]{3,1,2,0:T(8,128)}) fusion(f32[64,64,3,3]{1,0,3,2:T(8,128)S(1)} %copy-done.51, f32[64,66,2,7,2]{0,3,2,4,1:T(8,128)S(1)} %slice.518, f32[64,66,2,8,17]{0,3,2,4,1:T(8,128)S(1)} %copy.808, pred[16,17]{0,1:T(8,128)(4,1)S(1)} %copy-done.55), kind=kOutput, calls=%fused_computation.36 | convolution fusion | flops 3926640640 | bytes 14129424 | tf_op jit(solution)/shard_map/conv_general_dilated | solution.py:11
  208.6 9.7 copy.1001
  237.5 9.0 copy.926
  246.5 25.5 %all-gather.5.cloned.1.call-done = f32[16,2,2,64,192]{4,3,2,1,0:T(8,128)} async-done(((f32[1,2,2,64,192]{4,3,2,1,0:T(8,128)}), f32[16,2,2,64,192]{4,3,2,1,0:T(8,128)}) %all-gather.5.cloned.1.call-update) | async-done | bytes 3145744 | tf_op jit(solution)/shard_map/all_gather | solution.py:41
  285.8 28.1 %fusion.216 = f32[64,66,2,130]{0,2,3,1:T(2,128)S(1)} fusion(f32[2,64,1,130]{1,0,3,2:T(2,128)S(1)} %maximum_bitcast_fusion.4, f32[2,64,64,1]{1,0,3,2:T(2,128)S(1)} %slice_bitcast_fusion.13, f32[2,64,64,128]{1,0,3,2:T(2,128)} %bitcast.462, f32[2,64,64,1]{1,0,3,2:T(2,128)S(1)} %slice_bitcast_fusion.14, f32[2,64,1,130]{1,0,3,2:T(2,128)S(1)} %maximum_bitcast_fusion.3), kind=kLoop, calls=%fused_computation.507 | loop fusion | flops 4392960 | bytes 8785920 | tf_op jit(solution)/shard_map/jvp()/concatenate | solution.py:126
  318.4 63.1 %fusion.15 = (f32[64,16,17,64]{3,1,2,0:T(8,128)S(1)}, f32[64,16,17,64]{3,1,2,0:T(8,128)}) fusion(f32[64,64,3,3]{1,0,3,2:T(8,128)S(1)} %copy-done, f32[64,66,2,7,2]{0,3,2,4,1:T(8,128)S(1)} %slice.550, f32[64,66,2,8,17]{0,3,2,4,1:T(8,128)S(1)} %copy.827, pred[16,17]{0,1:T(8,128)(4,1)S(1)} %copy-done.55), kind=kOutput, calls=%fused_computation.38 | convolution fusion | flops 3926640640 | bytes 14129424 | tf_op jit(solution)/shard_map/jvp()/conv_general_dilated | solution.py:11
  387.7 12.2 %fusion.188 = (f32[64,2,128,64]{3,0,2,1:T(8,128)}, f32[2,64,64,128]{1,2,3,0:T(8,128)}) fusion(f32[64,2,136,64]{3,0,2,1:T(8,128)} %bitcast.464), kind=kLoop, calls=%fused_computation.488 | loop fusion | bytes 12582912 | tf_op jit(solution)/shard_map/mul | solution.py:15
  399.9 11.6 %copy.830 = f32[2,64,64,128]{1,3,2,0:T(8,128)} copy(f32[2,64,64,128]{1,2,3,0:T(8,128)} %get-tuple-element.63) | data formatting | bytes 8388608 | tf_op jit(solution)/shard_map/mul | solution.py:15
  418.6 25.3 %all_gather.14 = f32[16,2,2,64,48]{3,4,2,1,0:T(8,128)S(1)} all-gather(f32[1,2,2,64,48]{3,4,2,1,0:T(8,128)S(1)} %pad_maximum_fusion.7), channel_id=1, replica_groups=mesh['groups'=2,'face'=8,'tile'=2] {'face','tile'}, dimensions={0}, use_global_device_ids=true | all-gather | bytes 835584 | tf_op jit(solution)/shard_map/all_gather | solution.py:41
  470.3 8.8 copy.925
  479.1 10.5 broadcast_multiply_fusion
  524.6 9.3 copy.927
  538.9 32.1 %reduce-scatter.6.cloned.1.call-done = f32[1,2,2,64,48]{3,4,2,1,0:T(8,128)} async-done(((f32[16,2,2,64,48]{3,4,2,1,0:T(8,128)}), f32[1,2,2,64,48]{3,4,2,1,0:T(8,128)}) %reduce-scatter.6.cloned.1.call-update) | async-done | bytes 49168 | tf_op jit(solution)/shard_map/reduce_scatter | solution.py:49
  589.8 12.6 %fusion.39 = f32[2,64,64,128]{3,2,1,0:T(8,128)} fusion(f32[2,64,64,128]{3,2,1,0:T(8,128)} %get-tuple-element.193, f32[2,64,64,128]{3,2,1,0:T(8,128)} %copy.880, f32[2,64,64,128]{3,2,1,0:T(8,128)} %bitcast.474), kind=kLoop, calls=%fused_computation.84 | loop fusion | flops 75497472 | bytes 16777216 | tf_op jit(solution)/shard_map/transpose(jvp())/add_any | solution.py:15
  602.4 8.4 copy.881
  610.8 9.3 copy.941
  628.0 9.7 select_maximum_fusion.2
  637.7 11.3 %copy.883 = f32[64,64,2,8,19]{0,3,2,4,1:T(8,128)} copy(f32[64,64,2,8,19]{1,0,4,3,2:T(8,128)} %select_maximum_fusion.2) | data formatting | bytes 9961472 | tf_op jit(solution)/shard_map/transpose(jvp())/conv_general_dilated | solution.py:11
  649.0 25.5 %broadcast_select_fusion = f32[66,16,17,64]{3,1,2,0:T(8,128)} fusion(pred[16,17]{0,1:T(8,128)(4,1)S(1)} %copy-done.54, f32[64,64,3,3]{1,0,3,2:T(8,128)S(1)} %copy-done, f32[64,64,2,8,19]{0,3,2,4,1:T(8,128)} %copy.883), kind=kOutput, calls=%fused_computation.78 | convolution fusion | flops 3851520000 | bytes 9724176 | tf_op jit(solution)/shard_map/transpose(jvp())/conv_general_dilated | solution.py:11
  674.4 11.3 %copy.884 = f32[66,16,17,64]{0,3,2,1:T(8,128)} copy(f32[66,16,17,64]{3,1,2,0:T(8,128)} %broadcast_select_fusion) | data formatting | bytes 9191424 | tf_op jit(solution)/shard_map/transpose(jvp())/conv_general_dilated | solution.py:11
  686.7 8.6 slice.597
  695.3 11.4 %copy.935 = f32[66,2,130,64]{2,0,3,1:T(8,128)} copy(f32[66,2,130,64]{0,3,2,1:T(8,128)} %slice.597) | data formatting | bytes 8785920
  718.8 8.4 fusion.186
  755.4 93.1 %fusion.204 = f32[64,64,3,3]{0,1,3,2:T(8,128)} fusion(f32[2,64,64,128]{1,0,3,2:T(2,128)} %copy.881, f32[2,64,1,130]{1,0,3,2:T(2,128)S(1)} %copy-done.17, f32[2,64,64,1]{1,0,3,2:T(2,128)S(1)} %copy-done.27, f32[2,64,64,128]{1,0,3,2:T(2,128)} %bitcast.463, f32[2,64,64,1]{1,0,3,2:T(2,128)S(1)} %copy-done.29, f32[2,64,1,130]{1,0,3,2:T(2,128)S(1)} %copy-done.19), kind=kOutput, calls=%fused_computation.504 | convolution fusion | flops 3628271616 | bytes 8734720 | tf_op jit(solution)/shard_map/transpose(jvp())/conv_general_dilated | solution.py:11
  862.7 10.7 %fusion.43 = f32[2,64,64,128]{3,2,1,0:T(8,128)} fusion(f32[2,64,64,128]{3,2,1,0:T(8,128)S(1)} %slice_add_fusion, f32[2,64,64,128]{3,2,1,0:T(8,128)S(1)} %bitcast.473), kind=kLoop, calls=%fused_computation.88 | loop fusion | flops 74448896 | bytes 12582912 | tf_op jit(solution)/shard_map/transpose(jvp())/add_any | solution.py:15
  873.4 8.5 copy.903
  882.1 91.9 %fusion.205 = f32[3,3,64,64]{3,2,1,0:T(8,128)S(1)} fusion(f32[2,64,64,128]{1,0,3,2:T(2,128)} %copy.903, f32[2,64,1,130]{1,0,3,2:T(2,128)S(1)} %copy-done.13, f32[2,64,64,1]{1,0,3,2:T(2,128)S(1)} %copy-done.23, f32[2,64,64,128]{1,0,3,2:T(2,128)} %copy.804, f32[2,64,64,1]{1,0,3,2:T(2,128)S(1)} %copy-done.25, f32[2,64,1,130]{1,0,3,2:T(2,128)S(1)} %copy-done.15), kind=kOutput, calls=%fused_computation.505 | convolution fusion | flops 3628271616 | bytes 8734720 | tf_op jit(solution)/shard_map/transpose | solution.py:23
  978.5 50.8 %reduce-scatter.10.cloned.1.call-done = f32[1,18,128]{2,1,0:T(8,128)} async-done(((f32[16,18,128]{2,1,0:T(8,128)}), f32[1,18,128]{2,1,0:T(8,128)}) %reduce-scatter.10.cloned.1.call-update) | async-done | bytes 9232
  1029.3 20.2 %all_gather.15 = f32[16,18,128]{2,1,0:T(8,128)S(1)} all-gather(f32[1,18,128]{2,1,0:T(8,128)} %reduce-scatter.10.cloned.1.call-done), channel_id=1, replica_groups=mesh['groups'=2,'face'=8,'tile'=2] {'face','tile'}, dimensions={0}, use_global_device_ids=true | all-gather | bytes 156672 | tf_op jit(solution)/shard_map/all_gather | solution.py:26
  (388 shorter events, 253.3 us)
Async XLA Ops:
  7.2 311.2 %copy-start = (f32[64,64,3,3]{1,0,3,2:T(8,128)S(1)}, f32[64,64,3,3]{1,0,3,2:T(8,128)}, u32[]{:S(2)}) copy-start(f32[64,64,3,3]{1,0,3,2:T(8,128)} %param.11) | copy-start | bytes 442372
  7.2 70.0 %all-gather.3.cloned.1.call-start = ((), (), s32[]{:S(2)}) async-start(), calls=%async_computation.3 | async-start | bytes 4456448 | tf_op jit(solution)/shard_map/all_gather | solution.py:41
  23.6 248.4 %all-gather.5.cloned.1.call-start = ((), (), s32[]{:S(2)}) async-start(), calls=%async_computation.4 | async-start | bytes 4456448 | tf_op jit(solution)/shard_map/all_gather | solution.py:41
  23.6 8.4 copy-start.46
  23.6 8.5 copy-start.47
  34.7 411.5 %copy-start.43 = (pred[2,4,1]{0,1,2:T(4,128)(4,1)}, pred[2,4,1]{0,1,2:T(4,128)(4,1)S(1)}, u32[]{:S(2)}) copy-start(pred[2,4,1]{0,1,2:T(4,128)(4,1)S(1)} %copy.909) | copy-start | bytes 28
  90.2 29.8 %copy-start.22 = (f32[2,64,64,1]{1,0,3,2:T(2,128)}, f32[2,64,64,1]{1,0,3,2:T(2,128)S(1)}, u32[]{:S(2)}) copy-start(f32[2,64,64,1]{1,0,3,2:T(2,128)S(1)} %slice_bitcast_fusion.17) | copy-start | bytes 98308
  90.3 29.7 %copy-start.24 = (f32[2,64,64,1]{1,0,3,2:T(2,128)}, f32[2,64,64,1]{1,0,3,2:T(2,128)S(1)}, u32[]{:S(2)}) copy-start(f32[2,64,64,1]{1,0,3,2:T(2,128)S(1)} %slice_bitcast_fusion.18) | copy-start | bytes 98308
  91.7 28.3 %copy-start.12 = (f32[2,64,1,130]{1,0,3,2:T(2,128)}, f32[2,64,1,130]{1,0,3,2:T(2,128)S(1)}, u32[]{:S(2)}) copy-start(f32[2,64,1,130]{1,0,3,2:T(2,128)S(1)} %maximum_bitcast_fusion.2) | copy-start | bytes 199684
  91.8 28.2 %copy-start.14 = (f32[2,64,1,130]{1,0,3,2:T(2,128)}, f32[2,64,1,130]{1,0,3,2:T(2,128)S(1)}, u32[]{:S(2)}) copy-start(f32[2,64,1,130]{1,0,3,2:T(2,128)S(1)} %maximum_bitcast_fusion.1) | copy-start | bytes 199684
  208.6 14.3 %copy-start.2 = (s32[16]{0:T(128)S(1)}, s32[16]{0:T(128)}, u32[]{:S(2)}) copy-start(s32[16]{0:T(128)} %param.13) | copy-start | bytes 196
  222.8 348.3 %reduce-scatter.6.cloned.1.call-start = ((), (), s32[]{:S(2)}) async-start(), calls=%async_computation.5 | async-start | bytes 1671168 | tf_op jit(solution)/shard_map/reduce_scatter | solution.py:49
  285.2 28.8 %copy-start.26 = (f32[2,64,64,1]{1,0,3,2:T(2,128)}, f32[2,64,64,1]{1,0,3,2:T(2,128)S(1)}, u32[]{:S(2)}) copy-start(f32[2,64,64,1]{1,0,3,2:T(2,128)S(1)} %slice_bitcast_fusion.13) | copy-start | bytes 98308
  285.3 28.7 %copy-start.28 = (f32[2,64,64,1]{1,0,3,2:T(2,128)}, f32[2,64,64,1]{1,0,3,2:T(2,128)S(1)}, u32[]{:S(2)}) copy-start(f32[2,64,64,1]{1,0,3,2:T(2,128)S(1)} %slice_bitcast_fusion.14) | copy-start | bytes 98308
  285.7 28.3 %copy-start.16 = (f32[2,64,1,130]{1,0,3,2:T(2,128)}, f32[2,64,1,130]{1,0,3,2:T(2,128)S(1)}, u32[]{:S(2)}) copy-start(f32[2,64,1,130]{1,0,3,2:T(2,128)S(1)} %maximum_bitcast_fusion.4) | copy-start | bytes 199684
  285.8 28.2 %copy-start.18 = (f32[2,64,1,130]{1,0,3,2:T(2,128)}, f32[2,64,1,130]{1,0,3,2:T(2,128)S(1)}, u32[]{:S(2)}) copy-start(f32[2,64,1,130]{1,0,3,2:T(2,128)S(1)} %maximum_bitcast_fusion.3) | copy-start | bytes 199684
  470.3 8.8 copy-start.50
  513.9 334.6 %reduce-scatter.8.cloned.1.call-start = ((), (), s32[]{:S(2)}) async-start(), calls=%async_computation.6 | async-start | bytes 4456448 | tf_op jit(solution)/shard_map/reduce_scatter | solution.py:49
  524.6 9.3 copy-start.8
  524.6 9.3 copy-start.32
  524.6 9.3 copy-start.34
  524.6 9.3 copy-start.38
  524.6 9.3 copy-start.40
  637.7 11.3 %copy-start.54 = (pred[16,17]{0,1:T(8,128)(4,1)S(1)}, pred[16,17]{0,1:T(8,128)(4,1)}, u32[]{:S(2)}) copy-start(pred[16,17]{0,1:T(8,128)(4,1)} %constant.351) | copy-start | bytes 820
  727.2 10.1 copy-start.45
  754.4 220.4 %all-reduce.50.cloned.1.call-start = ((), (), s32[]{:S(2)}) async-start(), calls=%async_computation.8 | async-start | bytes 1179648 | tf_op jit(solution)/shard_map/psum | solution.py:223
  873.4 8.6 copy-start.13
  873.4 8.6 copy-start.15
  873.4 8.6 copy-start.23
  873.4 8.6 copy-start.25
  882.0 147.4 %reduce-scatter.10.cloned.1.call-start = ((), (), s32[]{:S(2)}) async-start(), calls=%async_computation.7 | async-start | bytes 208896
  882.1 168.4 %copy-start.1 = (f32[64,64,3,3]{1,0,3,2:T(8,128)S(1)}, f32[64,64,3,3]{1,0,3,2:T(8,128)}, u32[]{:S(2)}) copy-start(f32[64,64,3,3]{1,0,3,2:T(8,128)} %param.11) | copy-start | bytes 442372
  (34 other events, 105.4 us)
Sparse Core Ops, SparseCore 0:
  23.7 53.4 all-gather.2
  222.9 49.0 all-gather.4
  514.0 56.9 reduce-scatter.5
  754.5 71.3 reduce-scatter.7
  882.1 90.6 all-reduce.49
  976.7 52.5 reduce-scatter.9
where the time goes:
time: 1070 us; the launch traced here: 1060 us
  matrix products  358 us (33%)
  local copies, waits for them, and re-layouts  343 us (32%)
  waiting for transfers between devices  151 us (14%)
  other arithmetic  144 us (13%)
  blocking collectives  45.5 us (4%)
  between operations  16.2 us (2%)
    conv_general_dilated x7, matrix products, convolve(): lax.conv_general_dilated(padded, kernel, (1, 1), 'VALID', precision=lax.P...  266 us
    transpose x1, matrix products, split_sum(): turned = values.transpose(2, 3, 1, 0)  91.9 us
    unnamed x139, local copies, waits for them, and re-layouts  90.9 us
    all_gather x2, waiting for transfers between devices, fine_gather(): lax.all_gather(jnp.concatenate([columns, borders], axis=-1), ('face', 'ti...  68 us
    concatenate x3, other arithmetic, assemble(): jnp.concatenate([top_row[:, :, None], middle, bottom[:, :, None]], axis=2)  56.6 us
    conv_general_dilated x27, local copies, waits for them, and re-layouts, convolve(): lax.conv_general_dilated(padded, kernel, (1, 1), 'VALID', precision=lax.P...  56 us
    unnamed x7, waiting for transfers between devices  50.9 us
    mul x14, local copies, waits for them, and re-layouts, activate(): return jax.nn.gelu(values, approximate=False)  39 us
  transfers between devices with their start and end apart: 6, of which 4 were waited for; matrix products, arithmetic and copies ran while one was open for 24% of the time, Pallas kernels for 0%

commit v1 on v0

--- a/solution.py
+++ b/solution.py
@@ -38,9 +38,27 @@
 def fine_gather(tile_field):
     columns, borders = rim_pieces(tile_field)
     tile_rows = columns.shape[-1]
-    both = lax.all_gather(
-        jnp.concatenate([columns, borders], axis=-1), ("face", "tile"), axis=0, tiled=True
-    )
+    x = jnp.concatenate([columns, borders], axis=-1)
+    ways, here, step = (
+        lax.axis_size(("face", "tile")),
+        lax.axis_index(("face", "tile")),
+        x.shape[0],
+    )
+    shape = [n * ways if d == 0 else n for d, n in enumerate(x.shape)]
+    both = lax.dynamic_update_slice_in_dim(jnp.zeros(shape, x.dtype), x, here * step, axis=0)
+    going_up = going_down = x
+    for far in range(1, ways // 2 + 1):
+        going_up = lax.ppermute(
+            going_up, ("face", "tile"), [(d, (d + 1) % ways) for d in range(ways)]
+        )
+        both = lax.dynamic_update_slice_in_dim(both, going_up, (here - far) % ways * step, axis=0)
+        if 2 * far < ways:
+            going_down = lax.ppermute(
+                going_down, ("face", "tile"), [(d, (d - 1) % ways) for d in range(ways)]
+            )
+            both = lax.dynamic_update_slice_in_dim(
+                both, going_down, (here + far) % ways * step, axis=0
+            )
     return (both[..., :tile_rows], both[..., tile_rows:])
 
 

time: 1070 us -> 1200 us (1.12)
  starting transfers between devices: 0.25 us -> 99.6 us
  waiting for transfers between devices: 151 us -> 186 us
  blocking collectives: 45.5 us -> 20.2 us
  local copies, waits for them, and re-layouts: 343 us -> 366 us
    ppermute x0 -> x45, starting transfers between devices: none -> 99 us  [the longest x21 95.8 us: fine_gather(): lax.ppermute(going_down, ('face', 'tile'), [(d, (d - 1) % ways) for d in...]
    ppermute x0 -> x45, waiting for transfers between devices: none -> 84.4 us  [the longest x24 81.3 us: fine_gather(): lax.ppermute(going_up, ('face', 'tile'), [(d, (d + 1) % ways) for d in ra...]
    all_gather x2 -> x0, waiting for transfers between devices: 68 us -> none  [fine_gather(): lax.all_gather(jnp.concatenate([columns, borders], axis=-1), ('face', 'ti...]
    all_gather x1 -> x0, blocking collectives: 25.3 us -> none  [fine_gather(): lax.all_gather(jnp.concatenate([columns, borders], axis=-1), ('face', 'ti...]
    reduce_scatter x2, waiting for transfers between devices: 32.1 us -> 50.6 us  [fine_return(): lax.psum_scatter(jnp.concatenate([grad_columns, grad_borders], axis=-1),...]
    dynamic_update_slice x0 -> x46, local copies, waits for them, and re-layouts: none -> 13.2 us  [the longest x24 6.68 us: fine_gather(): lax.dynamic_update_slice_in_dim(both, going_up, (here - far) % ways * ste...]
    unnamed x139 -> x143, local copies, waits for them, and re-layouts: 90.9 us -> 88.7 us
    unnamed x7 -> x5, waiting for transfers between devices: 50.9 us -> 50.7 us
  transfers between devices with their start and end apart: 6 -> 49, of which waited for: 4 -> 30; matrix products, arithmetic and copies ran while one was open for 24% -> 23% of each run, Pallas kernels for 0% -> 0%
where the time goes in v1:
time: 1200 us; the launch traced here: 1190 us
  local copies, waits for them, and re-layouts  366 us (30%)
  matrix products  359 us (30%)
  waiting for transfers between devices  186 us (16%)
  other arithmetic  144 us (12%)
  starting transfers between devices  99.6 us (8%)
  blocking collectives  20.2 us (2%)
  between operations  16.8 us (1%)
    conv_general_dilated x7, matrix products, convolve(): lax.conv_general_dilated(padded, kernel, (1, 1), 'VALID', precision=lax.P...  267 us
    ppermute x21, starting transfers between devices, fine_gather(): lax.ppermute(going_down, ('face', 'tile'), [(d, (d - 1) % ways) for d in...  95.8 us
    transpose x1, matrix products, split_sum(): turned = values.transpose(2, 3, 1, 0)  92.1 us
    unnamed x143, local copies, waits for them, and re-layouts  88.7 us
    ppermute x24, waiting for transfers between devices, fine_gather(): lax.ppermute(going_up, ('face', 'tile'), [(d, (d + 1) % ways) for d in ra...  81.3 us
    concatenate x3, other arithmetic, assemble(): jnp.concatenate([top_row[:, :, None], middle, bottom[:, :, None]], axis=2)  56.6 us
    conv_general_dilated x27, local copies, waits for them, and re-layouts, convolve(): lax.conv_general_dilated(padded, kernel, (1, 1), 'VALID', precision=lax.P...  55.7 us
    unnamed x5, waiting for transfers between devices  50.7 us
  transfers between devices with their start and end apart: 49, of which 30 were waited for; matrix products, arithmetic and copies ran while one was open for 23% of the time, Pallas kernels for 0%

profile of v1, /device:TPU:0, one launch (start us, length us, event | category | flops | bytes accessed | tf_op | source)
XLA Modules:
  0.0 1190.6 jit_solution(5439815567765777399)
XLA Ops:
  8.6 8.1 fusion.189
  28.9 8.4 copy.1108
  125.4 28.1 %fusion.216 = f32[64,66,2,130]{0,2,3,1:T(2,128)S(1)} fusion(f32[2,64,1,130]{1,0,3,2:T(2,128)S(1)} %maximum_bitcast_fusion.2, f32[2,64,64,1]{1,0,3,2:T(2,128)S(1)} %slice_bitcast_fusion.17, f32[2,64,64,128]{1,0,3,2:T(2,128)} %copy.1108, f32[2,64,64,1]{1,0,3,2:T(2,128)S(1)} %slice_bitcast_fusion.18, f32[2,64,1,130]{1,0,3,2:T(2,128)S(1)} %maximum_bitcast_fusion.1), kind=kLoop, calls=%fused_computation.556 | loop fusion | flops 4392960 | bytes 8785920 | tf_op jit(solution)/shard_map/concatenate | solution.py:144
  158.2 72.1 %fusion.13 = (f32[64,16,17,64]{3,1,2,0:T(8,128)S(1)}, f32[64,16,17,64]{3,1,2,0:T(8,128)}) fusion(f32[64,64,3,3]{1,0,3,2:T(8,128)S(1)} %copy-done.53, f32[64,66,2,7,2]{0,3,2,4,1:T(8,128)S(1)} %slice.518, f32[64,66,2,8,17]{0,3,2,4,1:T(8,128)S(1)} %copy.1112, pred[16,17]{0,1:T(8,128)(4,1)S(1)} %copy-done.57), kind=kOutput, calls=%fused_computation.36 | convolution fusion | flops 3926640640 | bytes 14129424 | tf_op jit(solution)/shard_map/conv_general_dilated | solution.py:11
  242.2 9.7 copy.1335
  325.8 9.3 collective-permute-done.29
  348.7 28.1 %fusion.215 = f32[64,66,2,130]{0,2,3,1:T(2,128)S(1)} fusion(f32[2,64,1,130]{1,0,3,2:T(2,128)S(1)} %maximum_bitcast_fusion.4, f32[2,64,64,1]{1,0,3,2:T(2,128)S(1)} %slice_bitcast_fusion.13, f32[2,64,64,128]{1,0,3,2:T(2,128)} %bitcast.460, f32[2,64,64,1]{1,0,3,2:T(2,128)S(1)} %slice_bitcast_fusion.14, f32[2,64,1,130]{1,0,3,2:T(2,128)S(1)} %maximum_bitcast_fusion.3), kind=kLoop, calls=%fused_computation.555 | loop fusion | flops 4392960 | bytes 8785920 | tf_op jit(solution)/shard_map/jvp()/concatenate | solution.py:144
  381.3 63.0 %fusion.15 = (f32[64,16,17,64]{3,1,2,0:T(8,128)S(1)}, f32[64,16,17,64]{3,1,2,0:T(8,128)}) fusion(f32[64,64,3,3]{1,0,3,2:T(8,128)S(1)} %copy-done, f32[64,66,2,7,2]{0,3,2,4,1:T(8,128)S(1)} %slice.550, f32[64,66,2,8,17]{0,3,2,4,1:T(8,128)S(1)} %copy.1146, pred[16,17]{0,1:T(8,128)(4,1)S(1)} %copy-done.57), kind=kOutput, calls=%fused_computation.38 | convolution fusion | flops 3926640640 | bytes 14129424 | tf_op jit(solution)/shard_map/jvp()/conv_general_dilated | solution.py:11
  450.6 12.2 %fusion.187 = (f32[64,2,128,64]{3,0,2,1:T(8,128)}, f32[2,64,64,128]{1,2,3,0:T(8,128)}) fusion(f32[64,2,136,64]{3,0,2,1:T(8,128)} %bitcast.462), kind=kLoop, calls=%fused_computation.536 | loop fusion | bytes 12582912 | tf_op jit(solution)/shard_map/mul | solution.py:15
  462.8 11.6 copy.1149
  493.4 8.8 copy.1244
  506.6 9.2 copy.1243
  526.4 8.8 copy.1245
  605.0 8.0 copy.1167
  613.0 10.5 broadcast_multiply_fusion
  655.0 50.6 %reduce-scatter.6.cloned.1.call-done = f32[1,2,2,64,48]{3,4,2,1,0:T(8,128)} async-done(((f32[16,2,2,64,48]{3,4,2,1,0:T(8,128)}), f32[1,2,2,64,48]{3,4,2,1,0:T(8,128)}) %reduce-scatter.6.cloned.1.call-update) | async-done | bytes 49168 | tf_op jit(solution)/shard_map/reduce_scatter | solution.py:67
  724.3 12.7 %fusion.39 = f32[2,64,64,128]{3,2,1,0:T(8,128)} fusion(f32[2,64,64,128]{3,2,1,0:T(8,128)} %get-tuple-element.195, f32[2,64,64,128]{3,2,1,0:T(8,128)} %copy.1199, f32[2,64,64,128]{3,2,1,0:T(8,128)} %bitcast.472), kind=kLoop, calls=%fused_computation.84 | loop fusion | flops 75497472 | bytes 16777216 | tf_op jit(solution)/shard_map/transpose(jvp())/add_any | solution.py:15
  737.0 8.4 copy.1200
  745.4 9.2 copy.1259
  762.4 9.6 select_maximum_fusion.2
  772.1 11.3 copy.1202
  783.3 25.7 %broadcast_select_fusion = f32[66,16,17,64]{3,1,2,0:T(8,128)} fusion(pred[16,17]{0,1:T(8,128)(4,1)S(1)} %copy-done.56, f32[64,64,3,3]{1,0,3,2:T(8,128)S(1)} %copy-done, f32[64,64,2,8,19]{0,3,2,4,1:T(8,128)} %copy.1202), kind=kOutput, calls=%fused_computation.78 | convolution fusion | flops 3851520000 | bytes 9724176 | tf_op jit(solution)/shard_map/transpose(jvp())/conv_general_dilated | solution.py:11
  809.0 11.3 copy.1203
  821.3 8.5 slice.597
  829.8 11.2 copy.1253
  853.1 8.4 fusion.185
  889.2 92.9 %fusion.203 = f32[64,64,3,3]{0,1,3,2:T(8,128)} fusion(f32[2,64,64,128]{1,0,3,2:T(2,128)} %copy.1200, f32[2,64,1,130]{1,0,3,2:T(2,128)S(1)} %copy-done.15, f32[2,64,64,1]{1,0,3,2:T(2,128)S(1)} %copy-done.27, f32[2,64,64,128]{1,0,3,2:T(2,128)} %bitcast.461, f32[2,64,64,1]{1,0,3,2:T(2,128)S(1)} %copy-done.29, f32[2,64,1,130]{1,0,3,2:T(2,128)S(1)} %copy-done.17), kind=kOutput, calls=%fused_computation.552 | convolution fusion | flops 3628271616 | bytes 8734720 | tf_op jit(solution)/shard_map/transpose(jvp())/conv_general_dilated | solution.py:11
  996.1 10.7 fusion.43
  1006.8 8.4 copy.1222
  1015.3 92.1 %fusion.204 = f32[3,3,64,64]{3,2,1,0:T(8,128)S(1)} fusion(f32[2,64,64,128]{1,0,3,2:T(2,128)} %copy.1222, f32[2,64,1,130]{1,0,3,2:T(2,128)S(1)} %copy-done.11, f32[2,64,64,1]{1,0,3,2:T(2,128)S(1)} %copy-done.23, f32[2,64,64,128]{1,0,3,2:T(2,128)} %copy.1108, f32[2,64,64,1]{1,0,3,2:T(2,128)S(1)} %copy-done.25, f32[2,64,1,130]{1,0,3,2:T(2,128)S(1)} %copy-done.13), kind=kOutput, calls=%fused_computation.553 | convolution fusion | flops 3628271616 | bytes 8734720 | tf_op jit(solution)/shard_map/transpose | solution.py:23
  1111.9 50.6 %reduce-scatter.10.cloned.1.call-done = f32[1,18,128]{2,1,0:T(8,128)} async-done(((f32[16,18,128]{2,1,0:T(8,128)}), f32[1,18,128]{2,1,0:T(8,128)}) %reduce-scatter.10.cloned.1.call-update) | async-done | bytes 9232
  1162.5 20.2 %all_gather.3 = f32[16,18,128]{2,1,0:T(8,128)S(1)} all-gather(f32[1,18,128]{2,1,0:T(8,128)} %reduce-scatter.10.cloned.1.call-done), channel_id=1, replica_groups=mesh['groups'=2,'face'=8,'tile'=2] {'face','tile'}, dimensions={0}, use_global_device_ids=true | all-gather | bytes 156672 | tf_op jit(solution)/shard_map/all_gather | solution.py:26
  (538 shorter events, 435.8 us)
Async XLA Ops:
  7.2 698.4 %reduce-scatter.6.cloned.1.call-start = ((), (), s32[]{:S(2)}) async-start(), calls=%async_computation.3 | async-start | bytes 1671168 | tf_op jit(solution)/shard_map/reduce_scatter | solution.py:67
  22.8 22.5 %collective-permute-start = (f32[1,2,2,64,192]{4,3,1,2,0:T(8,128)S(1)}, f32[1,2,2,64,192]{4,3,1,2,0:T(8,128)S(1)}, u32[]{:S(2)}, u32[]{:S(2)}) collective-permute-start(f32[1,2,2,64,192]{4,3,1,2,0:T(8,128)S(1)} %pad_maximum_fusion.6), channel_id=1, source_target_pairs={{0,1},{1,2},{2,3},{3,4},{4,5},{5,6},{6,7},{7,8},{8,9},{9,10},{10,1... | collective-permute-start | bytes 589832 | tf_op jit(solution)/shard_map/ppermute | solution.py:51
  23.3 22.3 %collective-permute-start.1 = (f32[1,2,2,64,192]{4,3,1,2,0:T(8,128)S(1)}, f32[1,2,2,64,192]{4,3,1,2,0:T(8,128)S(1)}, u32[]{:S(2)}, u32[]{:S(2)}) collective-permute-start(f32[1,2,2,64,192]{4,3,1,2,0:T(8,128)S(1)} %pad_maximum_fusion.6), channel_id=1, source_target_pairs={{0,15},{1,0},{2,1},{3,2},{4,3},{5,4},{6,5},{7,6},{8,7},{9,8},{10,9... | collective-permute-start | bytes 589832 | tf_op jit(solution)/shard_map/ppermute | solution.py:56
  54.3 8.7 collective-permute-start.4
  54.6 8.6 collective-permute-start.5
  63.1 8.7 collective-permute-start.6
  63.4 8.6 collective-permute-start.7
  72.0 8.7 collective-permute-start.8
  72.2 8.6 collective-permute-start.9
  80.8 8.7 collective-permute-start.10
  89.9 8.8 collective-permute-start.13
  98.4 8.8 collective-permute-start.14
  255.4 10.0 collective-permute-start.15
  256.1 9.7 collective-permute-start.16
  265.4 9.9 collective-permute-start.17
  265.8 10.0 collective-permute-start.18
  275.3 10.0 collective-permute-start.19
  275.8 10.0 collective-permute-start.20
  285.3 10.0 collective-permute-start.21
  285.9 10.0 collective-permute-start.22
  295.3 10.0 collective-permute-start.23
  295.9 10.0 collective-permute-start.24
  305.3 10.0 collective-permute-start.25
  305.9 11.0 collective-permute-start.26
  315.3 10.0 collective-permute-start.27
  316.9 8.9 collective-permute-start.28
  325.3 9.9 collective-permute-start.29
  481.7 53.5 %collective-permute-start.30 = (f32[1,2,2,64,48]{3,4,2,1,0:T(8,128)S(1)}, f32[1,2,2,64,48]{3,4,2,1,0:T(8,128)S(1)}, u32[]{:S(2)}, u32[]{:S(2)}) collective-permute-start(f32[1,2,2,64,48]{3,4,2,1,0:T(8,128)S(1)} %get-tuple-element.130), channel_id=1, source_target_pairs={{0,1},{1,2},{2,3},{3,4},{4,5},{5,6},{6,7},{7,8},{8,9},{9,10},{10,1... | collective-permute-start | bytes 147464 | tf_op jit(solution)/shard_map/ppermute | solution.py:51
  502.2 33.2 %collective-permute-start.31 = (f32[1,2,2,64,48]{3,4,2,1,0:T(8,128)S(1)}, f32[1,2,2,64,48]{3,4,2,1,0:T(8,128)S(1)}, u32[]{:S(2)}, u32[]{:S(2)}) collective-permute-start(f32[1,2,2,64,48]{3,4,2,1,0:T(8,128)S(1)} %get-tuple-element.130), channel_id=1, source_target_pairs={{0,15},{1,0},{2,1},{3,2},{4,3},{5,4},{6,5},{7,6},{8,7},{9,8},{10,9... | collective-permute-start | bytes 147464 | tf_op jit(solution)/shard_map/ppermute | solution.py:56
  648.4 333.6 %reduce-scatter.8.cloned.1.call-start = ((), (), s32[]{:S(2)}) async-start(), calls=%async_computation.4 | async-start | bytes 4456448 | tf_op jit(solution)/shard_map/reduce_scatter | solution.py:67
  889.1 219.1 %all-reduce.50.cloned.1.call-start = ((), (), s32[]{:S(2)}) async-start(), calls=%async_computation.6 | async-start | bytes 1179648 | tf_op jit(solution)/shard_map/psum | solution.py:241
  1015.2 147.3 %reduce-scatter.10.cloned.1.call-start = ((), (), s32[]{:S(2)}) async-start(), calls=%async_computation.5 | async-start | bytes 208896
  (77 other events, 2656.2 us)
Sparse Core Ops, SparseCore 0:
  648.5 57.0 reduce-scatter.5
  889.2 71.3 reduce-scatter.7
  1015.3 90.5 all-reduce.49
  1109.9 52.5 reduce-scatter.9
